TPU v7x, 512 devices: a whole 4x4x16 slice. The times are simulated.
512 devices in a mesh: wave: 16 (over z), tile: 32 (over y, x, core).
Axes of the slice: x: 4, y: 4, z: 16, core: 2. Of those that a mesh axis runs over, the one named last changes fastest.
Arguments:
- warm_start: float32 [16, 2, 1024, 1024], P('wave', None, 'tile'), may hold values from -30 to 30
- class_map: int32 [1024, 1024], P('tile'), may hold values from 0 to 7
- conductivities: float32 [8], replicated, may hold values from 0.1 to 10
- wavenumbers: float32 [16], P('wave'), may hold values from 0.05 to 2
- weights: float32 [16], P('wave'), may hold values from 0.1 to 1
- source_row: int32 [2], replicated, may hold values from 0 to 1023
- source_col: int32 [2], replicated, may hold values from 0 to 1023
- electrode_row: int32 [64], replicated, may hold values from 0 to 1023
Outputs:
- potentials: float32 [2, 1024, 1024], P(None, 'tile', 'wave')
- readings: float32 [2, 64], replicated
All inputs are finite; a program needn't handle non-finite values.
Results may differ from a plain program's by a relative error of at most 0.0003.
Values sent between devices are 32-bit elements; how exact they have to be, the bound alone decides.
A program may use at most 64 MiB of HBM per device.

v0:
```python
import jax
import jax.numpy as jnp
from jax import lax
from jax.sharding import PartitionSpec as P

ITERS = 3
source_strength = 50.0


def extended(shard, sides, width):
    for axis, dim in sides:
        size, length = (lax.axis_size(axis), shard.shape[dim])
        up = [(i, (i + 1) % size) for i in range(size - 1)]
        down = [(j, i) for i, j in up]
        last = lax.slice_in_dim(shard, length - width, length, axis=dim)
        initial = lax.slice_in_dim(shard, 0, width, axis=dim)
        before = lax.ppermute(last, axis, up)
        after = lax.ppermute(initial, axis, down)
        shard = jnp.concatenate([before, shard, after], axis=dim)
    return shard


def harmonic(left_val, right_val):
    return 2.0 * left_val * right_val / (left_val + right_val)


def shards(
    warm_start,
    class_map,
    conductivities,
    wavenumbers,
    weights,
    source_row,
    source_col,
    electrode_row,
):
    rows_here = class_map.shape[0]
    depth = class_map.shape[1]
    n_class = conductivities.shape[0]
    class_ids = jnp.arange(n_class, dtype=jnp.int32)
    sigma = jnp.sum(
        jnp.where(class_map[None] == class_ids[:, None, None], conductivities[:, None, None], 0.0),
        axis=0,
    )
    sigma_rim = extended(sigma, (("tile", 0),), 1)
    face_row = harmonic(sigma_rim[:-1], sigma_rim[1:])
    face_up = face_row[:-1]
    face_down = face_row[1:]
    col_inner = harmonic(sigma[:, :-1], sigma[:, 1:])
    face_left = jnp.concatenate([jnp.zeros((rows_here, 1), jnp.float32), col_inner], axis=1)
    face_right = jnp.concatenate([col_inner, sigma[:, -1:]], axis=1)
    base = face_up + face_down + face_left + face_right
    wave_num = wavenumbers[0]
    diag = base + wave_num * wave_num * sigma
    global_row = lax.axis_index("tile") * rows_here + jnp.arange(rows_here, dtype=jnp.int32)
    col_ids = jnp.arange(depth, dtype=jnp.int32)
    hits = (global_row[None, :, None] == source_row[:, None, None]) & (
        col_ids[None, None, :] == source_col[:, None, None]
    )
    rhs = source_strength * hits.astype(jnp.float32)

    def operate(values):
        row_padded = extended(values, (("tile", 1),), 1)
        col_padded = jnp.pad(values, ((0, 0), (0, 0), (1, 1)))
        return (
            diag * values
            - face_up * row_padded[:, :-2]
            - face_down * row_padded[:, 2:]
            - face_left * col_padded[:, :, :-2]
            - face_right * col_padded[:, :, 2:]
        )

    def local_inner(first, second):
        return jnp.sum(first * second, axis=(1, 2))

    def resid_inner(residual, scaled):
        return lax.psum(local_inner(residual, scaled), "tile")[:, None, None]

    field = warm_start[0]
    residual = rhs - operate(field)
    scaled = residual / diag
    direction = scaled
    gamma_now = resid_inner(residual, scaled)
    for iteration in range(ITERS):
        image = operate(direction)
        curve = lax.psum(local_inner(direction, image), "tile")[:, None, None]
        step_size = gamma_now / curve
        field = field + step_size * direction
        residual = residual - step_size * image
        scaled = residual / diag
        gamma_next = resid_inner(residual, scaled)
        direction = scaled + gamma_next / gamma_now * direction
        gamma_now = gamma_next
    weighted = weights[0] * field
    picker = (global_row[:, None] == electrode_row[None, :]).astype(jnp.float32)
    local_read = jnp.dot(
        weighted[:, :, 0],
        picker,
        precision=lax.Precision.HIGHEST,
        preferred_element_type=jnp.float32,
    )
    readings = lax.psum(local_read, ("wave", "tile"))
    summed = lax.psum(weighted, "wave")
    share = depth // lax.axis_size("wave")
    potentials = lax.dynamic_slice_in_dim(summed, lax.axis_index("wave") * share, share, 2)
    return (potentials, readings)


def solution(mesh):
    return jax.shard_map(
        shards,
        mesh=mesh,
        in_specs=(
            P("wave", None, "tile", None),
            P("tile", None),
            P(),
            P("wave"),
            P("wave"),
            P(),
            P(),
            P(),
        ),
        out_specs=(P(None, "tile", "wave"), P()),
        check_vma=False,
    )
```

profile of v0, /device:TPU:2, one launch (start us, length us, event | category | flops | bytes accessed | tf_op | source)
XLA Modules:
  0.0 508.0 jit_solution(10058735618531560873)
XLA Ops:
  7.2 1.1 select_reduce_fusion
  8.3 1.9 collective-permute-start
  10.3 3.6 collective-permute-start.1
  13.9 1.9 collective-permute-start.2
  15.9 5.6 %collective-permute-start.3 = (f32[2,1,1024]{2,1,0:T(1,128)S(1)}, f32[2,1,1024]{2,1,0:T(1,128)S(1)}, u32[]{:S(2)}, u32[]{:S(2)}) collective-permute-start(f32[2,1,1024]{2,1,0:T(1,128)S(1)} %get-tuple-element.22), channel_id=1, source_target_pairs={{1,0},{2,1},{3,2},{4,3},{5,4},{6,5},{7,6},{8,7},{9,8},{10,9},{11,1... | collective-permute-start | bytes 24584 | tf_op jit(solution)/shard_map/ppermute | solution.py:18
  21.4 0.1 add_divide_fusion.1
  21.6 0.0 copy-start.2
  21.6 0.6 copy-done.2
  22.2 0.1 iota_compare_fusion.1
  22.3 0.6 copy-done.3
  22.9 0.1 broadcast_compare_fusion
  23.0 0.1 slice.146
  23.7 0.0 collective-permute-done
  23.7 0.0 collective-permute-done.1
  23.7 0.1 add_divide_fusion
  23.8 0.1 multiply_add_fusion.2
  23.9 0.2 broadcast_divide_fusion
  24.2 1.9 collective-permute-start.4
  26.1 3.6 collective-permute-start.5
  29.8 1.3 collective-permute-done.5
  31.1 0.3 multiply_reduce_fusion.3
  31.4 59.2 %all-reduce.5 = (f32[2]{0:T(128)S(1)}, f32[2]{0:T(128)S(1)}) all-reduce(f32[2]{0:T(128)S(1)} %get-tuple-element.3, f32[2]{0:T(128)S(1)} %get-tuple-element.2), channel_id=1, replica_groups=mesh['wave'=16,'tile'=32] {'tile'}, use_global_device_ids=true, to_apply=%region_2.3 | all-reduce | flops 4 | bytes 32 | tf_op jit(solution)/shard_map/psum | solution.py:77
  90.6 0.2 multiply_reduce_fusion.2
  90.8 62.7 %psum.58 = f32[2]{0:T(128)S(1)} all-reduce(f32[2]{0:T(128)S(1)} %get-tuple-element.8), channel_id=1, replica_groups=mesh['wave'=16,'tile'=32] {'tile'}, use_global_device_ids=true, to_apply=%region_6.7 | all-reduce | flops 2 | bytes 16 | tf_op jit(solution)/shard_map/psum | solution.py:77
  153.5 0.1 multiply_add_fusion.1
  153.6 1.9 collective-permute-start.6
  155.5 7.0 %collective-permute-start.7 = (f32[2,1,1024]{2,1,0:T(1,128)S(1)}, f32[2,1,1024]{2,1,0:T(1,128)S(1)}, u32[]{:S(2)}, u32[]{:S(2)}) collective-permute-start(f32[2,1,1024]{2,1,0:T(1,128)S(1)} %get-tuple-element.18), channel_id=1, source_target_pairs={{1,0},{2,1},{3,2},{4,3},{5,4},{6,5},{7,6},{8,7},{9,8},{10,9},{11,1... | collective-permute-start | bytes 24584 | tf_op jit(solution)/shard_map/ppermute | solution.py:18
  162.5 1.3 collective-permute-done.7
  163.8 0.3 multiply_reduce_fusion.1
  164.1 59.2 %psum.59 = f32[2]{0:T(128)S(1)} all-reduce(f32[2]{0:T(128)S(1)} %get-tuple-element.6), channel_id=1, replica_groups=mesh['wave'=16,'tile'=32] {'tile'}, use_global_device_ids=true, to_apply=%region_8.9 | all-reduce | flops 2 | bytes 16 | tf_op jit(solution)/shard_map/psum | solution.py:86
  223.3 0.2 multiply_reduce_fusion
  223.5 62.7 %psum.60 = f32[2]{0:T(128)S(1)} all-reduce(f32[2]{0:T(128)S(1)} %multiply_reduce_fusion), channel_id=1, replica_groups=mesh['wave'=16,'tile'=32] {'tile'}, use_global_device_ids=true, to_apply=%region_10.11 | all-reduce | flops 2 | bytes 16 | tf_op jit(solution)/shard_map/psum | solution.py:77
  286.2 0.1 multiply_add_fusion
  286.4 1.9 collective-permute-start.8
  288.3 7.0 %collective-permute-start.9 = (f32[2,1,1024]{2,1,0:T(1,128)S(1)}, f32[2,1,1024]{2,1,0:T(1,128)S(1)}, u32[]{:S(2)}, u32[]{:S(2)}) collective-permute-start(f32[2,1,1024]{2,1,0:T(1,128)S(1)} %get-tuple-element.16), channel_id=1, source_target_pairs={{1,0},{2,1},{3,2},{4,3},{5,4},{6,5},{7,6},{8,7},{9,8},{10,9},{11,1... | collective-permute-start | bytes 24584 | tf_op jit(solution)/shard_map/ppermute | solution.py:18
  295.3 1.3 collective-permute-done.9
  296.6 0.3 fusion.17
  297.6 59.2 %psum.61 = f32[2]{0:T(128)S(1)} all-reduce(f32[2]{0:T(128)S(1)} %fusion.17), channel_id=1, replica_groups=mesh['wave'=16,'tile'=32] {'tile'}, use_global_device_ids=true, to_apply=%region_12.13 | all-reduce | flops 2 | bytes 16 | tf_op jit(solution)/shard_map/psum | solution.py:86
  356.8 0.2 add_multiply_fusion
  357.0 0.1 slice_reduce_fusion
  357.1 0.6 copy-done
  357.7 0.1 all-reduce.8.cloned.1.call-update
  357.8 0.0 copy-start.4
  357.8 0.6 copy-done.4
  358.4 0.2 fusion.35
  358.6 110.4 %psum.63 = f32[2,64]{1,0:T(2,128)} all-reduce(f32[2,64]{1,0:T(2,128)S(1)} %fusion.35), channel_id=1, replica_groups=mesh['wave'=16,'tile'=32] {'wave','tile'}, use_global_device_ids=true, to_apply=%region_14.15 | all-reduce | flops 128 | bytes 1024 | tf_op jit(solution)/shard_map/psum | solution.py:102
  469.1 30.6 %all-reduce.8.cloned.1.call-done = f32[2,32,1024]{2,1,0:T(8,128)} async-done(((f32[2,32,1024]{2,1,0:T(8,128)}), f32[2,32,1024]{2,1,0:T(8,128)}) %all-reduce.8.cloned.1.call-update) | async-done | bytes 262160 | tf_op jit(solution)/shard_map/psum | solution.py:103
  499.7 1.4 constant_dynamic-slice_fusion
  (21 shorter events, 0.1 us)
Async XLA Ops:
  7.2 6.8 %copy-start.1 = (f32[1,2,32,1024]{3,2,1,0:T(8,128)S(1)}, f32[1,2,32,1024]{3,2,1,0:T(8,128)}, u32[]{:S(2)}) copy-start(f32[1,2,32,1024]{3,2,1,0:T(8,128)} %param.8) | copy-start | bytes 786436
  8.3 15.4 %collective-permute-start = (f32[1,1024]{1,0:T(1,128)S(1)}, f32[1,1024]{1,0:T(1,128)S(1)}, u32[]{:S(2)}, u32[]{:S(2)}) collective-permute-start(f32[1,1024]{1,0:T(1,128)S(1)} %get-tuple-element.26), channel_id=1, source_target_pairs={{0,1},{1,2},{2,3},{3,4},{4,5},{5,6},{6,7},{7,8},{8,9},{9,10},{10,1... | collective-permute-start | bytes 12296 | tf_op jit(solution)/shard_map/ppermute | solution.py:17
  10.3 13.4 %collective-permute-start.1 = (f32[1,1024]{1,0:T(1,128)S(1)}, f32[1,1024]{1,0:T(1,128)S(1)}, u32[]{:S(2)}, u32[]{:S(2)}) collective-permute-start(f32[1,1024]{1,0:T(1,128)S(1)} %get-tuple-element.27), channel_id=1, source_target_pairs={{1,0},{2,1},{3,2},{4,3},{5,4},{6,5},{7,6},{8,7},{9,8},{10,9},{11,1... | collective-permute-start | bytes 12296 | tf_op jit(solution)/shard_map/ppermute | solution.py:18
  13.9 9.9 %collective-permute-start.2 = (f32[2,1,1024]{2,1,0:T(1,128)S(1)}, f32[2,1,1024]{2,1,0:T(1,128)S(1)}, u32[]{:S(2)}, u32[]{:S(2)}) collective-permute-start(f32[2,1,1024]{2,1,0:T(1,128)S(1)} %get-tuple-element.21), channel_id=1, source_target_pairs={{0,1},{1,2},{2,3},{3,4},{4,5},{5,6},{6,7},{7,8},{8,9},{9,10},{10,1... | collective-permute-start | bytes 24584 | tf_op jit(solution)/shard_map/ppermute | solution.py:17
  15.9 8.0 %collective-permute-start.3 = (f32[2,1,1024]{2,1,0:T(1,128)S(1)}, f32[2,1,1024]{2,1,0:T(1,128)S(1)}, u32[]{:S(2)}, u32[]{:S(2)}) collective-permute-start(f32[2,1,1024]{2,1,0:T(1,128)S(1)} %get-tuple-element.22), channel_id=1, source_target_pairs={{1,0},{2,1},{3,2},{4,3},{5,4},{6,5},{7,6},{8,7},{9,8},{10,9},{11,1... | collective-permute-start | bytes 24584 | tf_op jit(solution)/shard_map/ppermute | solution.py:18
  21.6 0.7 copy-start.2
  22.2 0.7 copy-start.3
  24.2 5.6 %collective-permute-start.4 = (f32[2,1,1024]{2,1,0:T(1,128)S(1)}, f32[2,1,1024]{2,1,0:T(1,128)S(1)}, u32[]{:S(2)}, u32[]{:S(2)}) collective-permute-start(f32[2,1,1024]{2,1,0:T(1,128)S(1)} %get-tuple-element.19), channel_id=1, source_target_pairs={{0,1},{1,2},{2,3},{3,4},{4,5},{5,6},{6,7},{7,8},{8,9},{9,10},{10,1... | collective-permute-start | bytes 24584 | tf_op jit(solution)/shard_map/ppermute | solution.py:17
  26.1 5.0 collective-permute-start.5
  153.6 8.9 %collective-permute-start.6 = (f32[2,1,1024]{2,1,0:T(1,128)S(1)}, f32[2,1,1024]{2,1,0:T(1,128)S(1)}, u32[]{:S(2)}, u32[]{:S(2)}) collective-permute-start(f32[2,1,1024]{2,1,0:T(1,128)S(1)} %get-tuple-element.17), channel_id=1, source_target_pairs={{0,1},{1,2},{2,3},{3,4},{4,5},{5,6},{6,7},{7,8},{8,9},{9,10},{10,1... | collective-permute-start | bytes 24584 | tf_op jit(solution)/shard_map/ppermute | solution.py:17
  155.5 8.3 %collective-permute-start.7 = (f32[2,1,1024]{2,1,0:T(1,128)S(1)}, f32[2,1,1024]{2,1,0:T(1,128)S(1)}, u32[]{:S(2)}, u32[]{:S(2)}) collective-permute-start(f32[2,1,1024]{2,1,0:T(1,128)S(1)} %get-tuple-element.18), channel_id=1, source_target_pairs={{1,0},{2,1},{3,2},{4,3},{5,4},{6,5},{7,6},{8,7},{9,8},{10,9},{11,1... | collective-permute-start | bytes 24584 | tf_op jit(solution)/shard_map/ppermute | solution.py:18
  286.4 8.9 %collective-permute-start.8 = (f32[2,1,1024]{2,1,0:T(1,128)S(1)}, f32[2,1,1024]{2,1,0:T(1,128)S(1)}, u32[]{:S(2)}, u32[]{:S(2)}) collective-permute-start(f32[2,1,1024]{2,1,0:T(1,128)S(1)} %get-tuple-element.15), channel_id=1, source_target_pairs={{0,1},{1,2},{2,3},{3,4},{4,5},{5,6},{6,7},{7,8},{8,9},{9,10},{10,1... | collective-permute-start | bytes 24584 | tf_op jit(solution)/shard_map/ppermute | solution.py:17
  288.3 8.3 %collective-permute-start.9 = (f32[2,1,1024]{2,1,0:T(1,128)S(1)}, f32[2,1,1024]{2,1,0:T(1,128)S(1)}, u32[]{:S(2)}, u32[]{:S(2)}) collective-permute-start(f32[2,1,1024]{2,1,0:T(1,128)S(1)} %get-tuple-element.16), channel_id=1, source_target_pairs={{1,0},{2,1},{3,2},{4,3},{5,4},{6,5},{7,6},{8,7},{9,8},{10,9},{11,1... | collective-permute-start | bytes 24584 | tf_op jit(solution)/shard_map/ppermute | solution.py:18
  357.0 0.7 copy-start
  357.1 142.7 %all-reduce.8.cloned.1.call-start = ((), (), s32[]{:S(2)}) async-start(), calls=%async_computation | async-start | bytes 524288 | tf_op jit(solution)/shard_map/psum | solution.py:103
  357.8 0.7 copy-start.4
Sparse Core Ops, SparseCore 0:
  360.2 139.4 all-reduce.7
where the time goes:
time: 509 us; the launch traced here: 508 us
  blocking collectives  413 us (81%)
  starting transfers between devices  36.4 us (7%)
  waiting for transfers between devices  34.8 us (7%)
  between operations  15.6 us (3%)
    psum x3, blocking collectives, resid_inner(): return lax.psum(local_inner(residual, scaled), 'tile')[:, None, None]  184 us
    psum x2, blocking collectives, shards(): curve = lax.psum(local_inner(direction, image), 'tile')[:, None, None]  118 us
    psum x1, blocking collectives, shards(): readings = lax.psum(local_read, ('wave', 'tile'))  110 us
    psum x1, waiting for transfers between devices, shards(): summed = lax.psum(weighted, 'wave')  30.6 us
    ppermute x5, starting transfers between devices, extended(): after = lax.ppermute(initial, axis, down)  26.8 us
  transfers between devices with their start and end apart: 11, of which 4 were waited for; matrix products, arithmetic and copies ran while one was open for 0% of the time, Pallas kernels for 0%

commit v1 on v0

--- a/solution.py
+++ b/solution.py
@@ -100,7 +100,9 @@
         preferred_element_type=jnp.float32,
     )
     readings = lax.psum(local_read, ("wave", "tile"))
-    summed = lax.psum(weighted, "wave")
+    summed = weighted
+    for hop in (1, 2, 4, 8):
+        summed = summed + lax.ppermute(summed, "wave", [(dev, dev ^ hop) for dev in range(16)])
     share = depth // lax.axis_size("wave")
     potentials = lax.dynamic_slice_in_dim(summed, lax.axis_index("wave") * share, share, 2)
     return (potentials, readings)

time: 509 us -> 529 us (1.039)
  the two profiles are of different devices: /device:TPU:2 before, /device:TPU:1 now
where the time goes in v1:
time: 529 us
  blocking collectives  412 us (78%)
  starting transfers between devices  62.7 us (12%)
  waiting for transfers between devices  46 us (9%)
    psum x3, blocking collectives, resid_inner(): return lax.psum(local_inner(residual, scaled), 'tile')[:, None, None]  190 us
    psum x2, blocking collectives, shards(): curve = lax.psum(local_inner(direction, image), 'tile')[:, None, None]  121 us
    psum x1, blocking collectives, shards(): readings = lax.psum(local_read, ('wave', 'tile'))  101 us
    ppermute x4, waiting for transfers between devices, shards(): lax.ppermute(summed, 'wave', [(dev, dev ^ hop) for dev in range(16)])  37.7 us
    ppermute x4, starting transfers between devices, shards(): lax.ppermute(summed, 'wave', [(dev, dev ^ hop) for dev in range(16)])  34.7 us
    ppermute x5, starting transfers between devices, extended(): after = lax.ppermute(initial, axis, down)  14.7 us
    ppermute x5, starting transfers between devices, extended(): before = lax.ppermute(last, axis, up)  13.3 us
  transfers between devices with their start and end apart: 14, of which 7 were waited for; matrix products, arithmetic and copies ran while one was open for 0% of the time, Pallas kernels for 0%

profile of v1, /device:TPU:1, one launch (start us, length us, event | category | flops | bytes accessed | tf_op | source)
XLA Modules:
  0.0 528.8 jit_solution(2274133457379855286)
XLA Ops:
  0.6 1.1 select_reduce_fusion
  1.8 4.5 collective-permute-start
  6.3 5.6 %collective-permute-start.1 = (f32[1,1024]{1,0:T(1,128)S(1)}, f32[1,1024]{1,0:T(1,128)S(1)}, u32[]{:S(2)}, u32[]{:S(2)}) collective-permute-start(f32[1,1024]{1,0:T(1,128)S(1)} %get-tuple-element.27), channel_id=1, source_target_pairs={{1,0},{2,1},{3,2},{4,3},{5,4},{6,5},{7,6},{8,7},{9,8},{10,9},{11,1... | collective-permute-start | bytes 12296 | tf_op jit(solution)/shard_map/ppermute | solution.py:18
  11.9 1.9 collective-permute-start.2
  13.9 2.4 collective-permute-start.3
  16.3 0.1 add_divide_fusion.1
  16.4 0.6 copy-done.1
  17.0 0.1 iota_compare_fusion.1
  17.1 0.6 copy-done.2
  17.7 0.1 broadcast_compare_fusion
  17.8 0.1 slice.146
  18.6 0.1 multiply_add_fusion.2
  18.7 0.1 collective-permute-done.3
  18.8 0.2 broadcast_divide_fusion
  19.1 3.1 collective-permute-start.4
  22.2 1.9 collective-permute-start.5
  24.1 3.0 collective-permute-done.5
  27.1 0.3 multiply_reduce_fusion.3
  27.4 60.1 %all-reduce.5 = (f32[2]{0:T(128)S(1)}, f32[2]{0:T(128)S(1)}) all-reduce(f32[2]{0:T(128)S(1)} %get-tuple-element.3, f32[2]{0:T(128)S(1)} %get-tuple-element.2), channel_id=1, replica_groups=mesh['wave'=16,'tile'=32] {'tile'}, use_global_device_ids=true, to_apply=%region_2.3 | all-reduce | flops 4 | bytes 32 | tf_op jit(solution)/shard_map/psum | solution.py:77
  87.6 0.2 multiply_reduce_fusion.2
  87.8 65.1 %psum.51 = f32[2]{0:T(128)S(1)} all-reduce(f32[2]{0:T(128)S(1)} %get-tuple-element.8), channel_id=1, replica_groups=mesh['wave'=16,'tile'=32] {'tile'}, use_global_device_ids=true, to_apply=%region_6.7 | all-reduce | flops 2 | bytes 16 | tf_op jit(solution)/shard_map/psum | solution.py:77
  152.8 0.1 multiply_add_fusion.1
  153.0 1.9 collective-permute-start.6
  154.9 2.4 collective-permute-start.7
  157.3 2.5 collective-permute-done.7
  159.9 0.3 multiply_reduce_fusion.1
  160.2 60.6 %psum.52 = f32[2]{0:T(128)S(1)} all-reduce(f32[2]{0:T(128)S(1)} %get-tuple-element.6), channel_id=1, replica_groups=mesh['wave'=16,'tile'=32] {'tile'}, use_global_device_ids=true, to_apply=%region_8.9 | all-reduce | flops 2 | bytes 16 | tf_op jit(solution)/shard_map/psum | solution.py:86
  220.8 0.2 multiply_reduce_fusion
  221.0 64.6 %psum.53 = f32[2]{0:T(128)S(1)} all-reduce(f32[2]{0:T(128)S(1)} %multiply_reduce_fusion), channel_id=1, replica_groups=mesh['wave'=16,'tile'=32] {'tile'}, use_global_device_ids=true, to_apply=%region_10.11 | all-reduce | flops 2 | bytes 16 | tf_op jit(solution)/shard_map/psum | solution.py:77
  285.6 0.1 multiply_add_fusion
  285.7 1.9 collective-permute-start.8
  287.7 2.4 collective-permute-start.9
  290.1 2.5 collective-permute-done.9
  292.6 0.3 fusion.17
  293.6 60.6 %psum.54 = f32[2]{0:T(128)S(1)} all-reduce(f32[2]{0:T(128)S(1)} %fusion.17), channel_id=1, replica_groups=mesh['wave'=16,'tile'=32] {'tile'}, use_global_device_ids=true, to_apply=%region_12.13 | all-reduce | flops 2 | bytes 16 | tf_op jit(solution)/shard_map/psum | solution.py:86
  354.2 0.1 add_multiply_fusion
  354.4 3.1 collective-permute-start.10
  357.5 4.0 collective-permute-done.10
  361.5 4.6 collective-permute-start.11
  366.2 11.1 %collective-permute-done.11 = f32[2,32,1024]{2,1,0:T(8,128)S(1)} collective-permute-done((f32[2,32,1024]{2,1,0:T(8,128)S(1)}, f32[2,32,1024]{2,1,0:T(8,128)S(1)}, u32[]{:S(2)}, u32[]{:S(2)}) %collective-permute-start.11) | collective-permute-done | bytes 262176 | tf_op jit(solution)/shard_map/ppermute | solution.py:105
  377.3 8.8 %collective-permute-start.12 = (f32[2,32,1024]{2,1,0:T(8,128)S(1)}, f32[2,32,1024]{2,1,0:T(8,128)S(1)}, u32[]{:S(2)}, u32[]{:S(2)}) collective-permute-start(f32[2,32,1024]{2,1,0:T(8,128)S(1)} %add.100), channel_id=1, source_target_pairs={{0,128},{32,160},{64,192},{96,224},{128,0},{160,32},{192,64},{224,... | collective-permute-start | bytes 786440 | tf_op jit(solution)/shard_map/ppermute | solution.py:105
  386.2 22.6 %collective-permute-done.12 = f32[2,32,1024]{2,1,0:T(8,128)S(1)} collective-permute-done((f32[2,32,1024]{2,1,0:T(8,128)S(1)}, f32[2,32,1024]{2,1,0:T(8,128)S(1)}, u32[]{:S(2)}, u32[]{:S(2)}) %collective-permute-start.12) | collective-permute-done | bytes 262176 | tf_op jit(solution)/shard_map/ppermute | solution.py:105
  408.8 0.0 copy-start.3
  408.8 18.2 %collective-permute-start.13 = (f32[2,32,1024]{2,1,0:T(8,128)S(1)}, f32[2,32,1024]{2,1,0:T(8,128)S(1)}, u32[]{:S(2)}, u32[]{:S(2)}) collective-permute-start(f32[2,32,1024]{2,1,0:T(8,128)S(1)} %add.101), channel_id=1, source_target_pairs={{0,256},{32,288},{64,320},{96,352},{128,384},{160,416},{192,448},{... | collective-permute-start | bytes 786440 | tf_op jit(solution)/shard_map/ppermute | solution.py:105
  427.0 0.1 slice_reduce_fusion
  427.1 0.2 fusion.35
  427.3 100.8 %psum.55 = f32[2,64]{1,0:T(2,128)} all-reduce(f32[2,64]{1,0:T(2,128)S(1)} %fusion.35), channel_id=1, replica_groups=mesh['wave'=16,'tile'=32] {'wave','tile'}, use_global_device_ids=true, to_apply=%region_13.14 | all-reduce | flops 128 | bytes 1024 | tf_op jit(solution)/shard_map/psum | solution.py:102
  528.1 0.7 dynamic-slice_add_fusion
  (27 shorter events, 0.3 us)
Async XLA Ops:
  0.6 11.3 %copy-start = (f32[1,2,32,1024]{3,2,1,0:T(8,128)S(1)}, f32[1,2,32,1024]{3,2,1,0:T(8,128)}, u32[]{:S(2)}) copy-start(f32[1,2,32,1024]{3,2,1,0:T(8,128)} %param.8) | copy-start | bytes 786436
  1.8 16.7 %collective-permute-start = (f32[1,1024]{1,0:T(1,128)S(1)}, f32[1,1024]{1,0:T(1,128)S(1)}, u32[]{:S(2)}, u32[]{:S(2)}) collective-permute-start(f32[1,1024]{1,0:T(1,128)S(1)} %get-tuple-element.26), channel_id=1, source_target_pairs={{0,1},{1,2},{2,3},{3,4},{4,5},{5,6},{6,7},{7,8},{8,9},{9,10},{10,1... | collective-permute-start | bytes 12296 | tf_op jit(solution)/shard_map/ppermute | solution.py:17
  6.3 12.2 %collective-permute-start.1 = (f32[1,1024]{1,0:T(1,128)S(1)}, f32[1,1024]{1,0:T(1,128)S(1)}, u32[]{:S(2)}, u32[]{:S(2)}) collective-permute-start(f32[1,1024]{1,0:T(1,128)S(1)} %get-tuple-element.27), channel_id=1, source_target_pairs={{1,0},{2,1},{3,2},{4,3},{5,4},{6,5},{7,6},{8,7},{9,8},{10,9},{11,1... | collective-permute-start | bytes 12296 | tf_op jit(solution)/shard_map/ppermute | solution.py:18
  11.9 6.8 %collective-permute-start.2 = (f32[2,1,1024]{2,1,0:T(1,128)S(1)}, f32[2,1,1024]{2,1,0:T(1,128)S(1)}, u32[]{:S(2)}, u32[]{:S(2)}) collective-permute-start(f32[2,1,1024]{2,1,0:T(1,128)S(1)} %get-tuple-element.21), channel_id=1, source_target_pairs={{0,1},{1,2},{2,3},{3,4},{4,5},{5,6},{6,7},{7,8},{8,9},{9,10},{10,1... | collective-permute-start | bytes 24584 | tf_op jit(solution)/shard_map/ppermute | solution.py:17
  13.9 5.0 collective-permute-start.3
  16.4 0.7 copy-start.1
  17.0 0.7 copy-start.2
  19.1 5.0 collective-permute-start.4
  22.2 5.0 collective-permute-start.5
  153.0 4.3 collective-permute-start.6
  154.9 5.0 collective-permute-start.7
  285.7 4.3 collective-permute-start.8
  287.7 5.0 collective-permute-start.9
  354.4 7.1 %collective-permute-start.10 = (f32[2,32,1024]{2,1,0:T(8,128)S(1)}, f32[2,32,1024]{2,1,0:T(8,128)S(1)}, u32[]{:S(2)}, u32[]{:S(2)}) collective-permute-start(f32[2,32,1024]{2,1,0:T(8,128)S(1)} %add_multiply_fusion), channel_id=1, source_target_pairs={{0,32},{32,0},{64,96},{96,64},{128,160},{160,128},{192,224},{224,1... | collective-permute-start | bytes 786440 | tf_op jit(solution)/shard_map/ppermute | solution.py:105
  361.5 15.8 %collective-permute-start.11 = (f32[2,32,1024]{2,1,0:T(8,128)S(1)}, f32[2,32,1024]{2,1,0:T(8,128)S(1)}, u32[]{:S(2)}, u32[]{:S(2)}) collective-permute-start(f32[2,32,1024]{2,1,0:T(8,128)S(1)} %add.99), channel_id=1, source_target_pairs={{0,64},{32,96},{64,0},{96,32},{128,192},{160,224},{192,128},{224,1... | collective-permute-start | bytes 786440 | tf_op jit(solution)/shard_map/ppermute | solution.py:105
  377.3 31.4 %collective-permute-start.12 = (f32[2,32,1024]{2,1,0:T(8,128)S(1)}, f32[2,32,1024]{2,1,0:T(8,128)S(1)}, u32[]{:S(2)}, u32[]{:S(2)}) collective-permute-start(f32[2,32,1024]{2,1,0:T(8,128)S(1)} %add.100), channel_id=1, source_target_pairs={{0,128},{32,160},{64,192},{96,224},{128,0},{160,32},{192,64},{224,... | collective-permute-start | bytes 786440 | tf_op jit(solution)/shard_map/ppermute | solution.py:105
  408.8 18.3 %copy-start.3 = (s32[64]{0:T(128)S(1)}, s32[64]{0:T(128)}, u32[]{:S(2)}) copy-start(s32[64]{0:T(128)} %param.15) | copy-start | bytes 772
  408.8 119.3 %collective-permute-start.13 = (f32[2,32,1024]{2,1,0:T(8,128)S(1)}, f32[2,32,1024]{2,1,0:T(8,128)S(1)}, u32[]{:S(2)}, u32[]{:S(2)}) collective-permute-start(f32[2,32,1024]{2,1,0:T(8,128)S(1)} %add.101), channel_id=1, source_target_pairs={{0,256},{32,288},{64,320},{96,352},{128,384},{160,416},{192,448},{... | collective-permute-start | bytes 786440 | tf_op jit(solution)/shard_map/ppermute | solution.py:105
